TPU v7x, 256 devices: a whole 4x4x8 slice. The times are simulated.
256 devices in a mesh: outer: 8 (over x_hi, y), inner: 32 (over x_lo, z, core).
Axes of the slice: x: 4 (x_hi: 2, x_lo: 2; x = x_hi * 2 + x_lo), y: 4, z: 8, core: 2. Of those that a mesh axis runs over, the one named last changes fastest.
Arguments:
- queries: bfloat16 [49152, 4096], P(('outer', 'inner'))
- keys: bfloat16 [49152, 1024], P(('outer', 'inner'))
- values: bfloat16 [49152, 1024], P(('outer', 'inner')), may hold values from -6 to 6
- stretch_of: int32 [8, 32, 2], replicated, may hold values from 0 to 511, as said below
Outputs:
- attended: bfloat16 [49152, 4096], P(('outer', 'inner'))
Inputs may be any that keep to these rules, and one draw needn't show every extreme that they name: There is a permutation P of 0 to 7 with stretch_of[g, s] = (2 * 32 * P(g) + s, 2 * 32 * P(g) + 2 * 32 - 1 - s).
All inputs are finite; a program needn't handle non-finite values.
Results may differ from a plain program's by a relative error of at most 0.0095.
Values may be sent and summed in bfloat16 or wider, within the bound.
A program may use at most 64 MiB of HBM per device.

v0:
```python
import jax
import jax.numpy as jnp
from jax import lax
from jax.sharding import PartitionSpec as P

QUERY_HEADS = 32
KEY_VALUE_HEADS = 8
HEAD_SIZE = 128


def from_behind(block, axis, distance):
    devices = range(lax.axis_size(axis))
    route = [((i - distance) % len(devices), i) for i in devices]
    return lax.ppermute(block, axis, route)


def on_device(queries, keys, values, stretch_of):
    token_rows = queries.shape[0]
    stretch_rows = token_rows // 2
    shard_pieces = lax.axis_size("inner")
    query_groups = lax.axis_size("outer")
    group_now = lax.axis_index("outer")
    shard_now = lax.axis_index("inner")
    score_scale = HEAD_SIZE ** (-0.5)
    offsets = jnp.arange(stretch_rows, dtype=jnp.int32)

    def positions(group, shard):
        stretches = stretch_of[group, shard]
        return (stretches[:, None] * stretch_rows + offsets[None, :]).reshape(token_rows)

    paired = jnp.stack((keys, values))
    blocks = [(paired, positions(group_now, shard_now))]
    moving = paired
    for stride in range(1, 4):
        moving = from_behind(moving, "inner", 1)
        blocks.append((moving, positions(group_now, (shard_now - stride) % shard_pieces)))
    remote = from_behind(paired, "outer", 1)
    blocks.append((remote, positions((group_now - 1) % query_groups, shard_now)))
    grouped_query = queries.reshape(
        token_rows, KEY_VALUE_HEADS, QUERY_HEADS // KEY_VALUE_HEADS, HEAD_SIZE
    )
    query_pos = blocks[0][1]
    score_list = []
    for key_value_block, key_pos in blocks:
        key_matrix = key_value_block[0].reshape(token_rows, KEY_VALUE_HEADS, HEAD_SIZE)
        scores = (
            jnp.einsum(
                "tkgd,ukd->kgtu", grouped_query, key_matrix, preferred_element_type=jnp.float32
            )
            * score_scale
        )
        visible = key_pos[None, :] <= query_pos[:, None]
        score_list.append(jnp.where(visible, scores, -jnp.inf))
    row_max = jnp.max(score_list[0], axis=-1, keepdims=True)
    for scores in score_list[1:]:
        row_max = jnp.maximum(row_max, jnp.max(scores, axis=-1, keepdims=True))
    row_sum = jnp.zeros(row_max.shape, jnp.float32)
    running_total = jnp.zeros(
        (KEY_VALUE_HEADS, QUERY_HEADS // KEY_VALUE_HEADS, token_rows, HEAD_SIZE), jnp.float32
    )
    for scores, (key_value_block, key_pos) in zip(score_list, blocks):
        weights = jnp.exp(scores - row_max)
        row_sum = row_sum + jnp.sum(weights, axis=-1, keepdims=True)
        rounded = weights.astype(jnp.bfloat16)
        value_matrix = key_value_block[1].reshape(token_rows, KEY_VALUE_HEADS, HEAD_SIZE)
        running_total = running_total + jnp.einsum(
            "kgtu,ukd->kgtd", rounded, value_matrix, preferred_element_type=jnp.float32
        )
    weighted = running_total / row_sum
    return (
        weighted.transpose(2, 0, 1, 3)
        .reshape(token_rows, QUERY_HEADS * HEAD_SIZE)
        .astype(jnp.bfloat16)
    )


def solution(mesh):
    in_specs = (
        P(("outer", "inner"), None),
        P(("outer", "inner"), None),
        P(("outer", "inner"), None),
        P(),
    )
    out_specs = P(("outer", "inner"), None)
    return jax.shard_map(
        on_device, mesh=mesh, in_specs=in_specs, out_specs=out_specs, check_vma=False
    )
```

profile of v0, /device:TPU:2, one launch (start us, length us, event | category | flops | bytes accessed | tf_op | source)
XLA Modules:
  0.0 96.3 jit_solution(8688300169541580848)
XLA Ops:
  0.0 1.2 %pad_maximum_fusion = bf16[2,192,1024]{2,1,0:T(8,128)(2,1)S(1)} fusion(bf16[1,192,1024]{2,1,0:T(8,128)(2,1)} %bitcast.124, bf16[1,192,1024]{2,1,0:T(8,128)(2,1)} %bitcast.122), kind=kLoop, calls=%fused_computation.62 | loop fusion | flops 393216 | bytes 1572864 | tf_op jit(solution)/shard_map/stack | solution.py:31
  1.3 1.7 %collective-permute-start.3 = (bf16[2,192,1024]{2,1,0:T(8,128)(2,1)S(1)}, bf16[2,192,1024]{2,1,0:T(8,128)(2,1)}, u32[]{:S(2)}, u32[]{:S(2)}) collective-permute-start(bf16[2,192,1024]{2,1,0:T(8,128)(2,1)S(1)} %pad_maximum_fusion), channel_id=1, source_target_pairs={{224,0},{0,32},{32,64},{64,96},{96,128},{128,160},{160,192},{192,2... | collective-permute-start | bytes 2359304 | tf_op jit(solution)/shard_map/ppermute | solution.py:14
  2.9 1.1 %fusion.71 = (s32[2]{0:T(128)S(1)}, s32[2]{0:T(128)S(1)}, s32[2]{0:T(128)S(1)}, s32[2]{0:T(128)S(1)}, s32[2]{0:T(128)S(1)}) fusion(s32[8,32,2]{1,2,0:T(2,128)} %param.7, s32[]{:T(128)S(6)} %select_n.57, s32[]{:T(128)S(6)} %select_n.61, s32[]{:T(128)S(6)} %select_n.64, s32[]{:T(128)S(6)} %select_n.58, s32[]{:T(128)S(6)} %select_n.70, s32[]{:T(128)S(6)} %select_n.67), kind=kLoop, calls=%fused_computation.96 | loop fusion | flops 10 | bytes 104 | tf_op jit(solution)/shard_map/mul | solution.py:29
  4.7 2.8 %reshape.169 = bf16[192,8,4,128]{3,2,1,0:T(4,128)(2,1)S(1)} reshape(bf16[192,4096]{1,0:T(8,128)(2,1)} %param.4) | data formatting | bytes 3145728 | tf_op jit(solution)/shard_map/reshape | solution.py:39
  7.5 1.1 %copy.73 = bf16[24,8,8,128]{3,2,1,0:T(8,128)(2,1)S(1)} copy(bf16[24,8,8,128]{3,1,2,0:T(8,128)(2,1)} %bitcast.123) | data formatting | bytes 786432
  8.6 1.1 %copy.78 = bf16[24,8,8,128]{3,2,1,0:T(8,128)(2,1)S(1)} copy(bf16[24,8,8,128]{3,1,2,0:T(8,128)(2,1)} %bitcast.125) | data formatting | bytes 786432
  9.8 1.7 %fusion.10 = (f32[8,4,192]{2,1,0:T(4,128)S(1)}, f32[8,192,192,4]{2,1,3,0:T(8,128)S(1)}) fusion(pred[192,192]{0,1:T(8,128)(4,1)S(1)} %get-tuple-element.27, bf16[192,8,4,128]{3,2,1,0:T(4,128)(2,1)S(1)} %reshape.169, bf16[192,8,128,1]{2,1,0,3:T(8,128)(2,1)S(1)} %bitcast.118), kind=kOutput, calls=%fused_computation.20 | convolution fusion | flops 305522688 | bytes 6746112 | tf_op jit(solution)/shard_map/tkgd,ukd->kgtu/dot_general | solution.py:47
  11.6 4.7 %collective-permute-done = bf16[2,192,1024]{2,1,0:T(8,128)(2,1)S(1)} collective-permute-done((bf16[2,192,1024]{2,1,0:T(8,128)(2,1)S(1)}, bf16[2,192,1024]{2,1,0:T(8,128)(2,1)S(1)}, u32[]{:S(2)}, u32[]{:S(2)}) %collective-permute-start) | collective-permute-done | bytes 786464 | tf_op jit(solution)/shard_map/ppermute | solution.py:14
  16.2 25.2 %collective-permute-done.3 = bf16[2,192,1024]{2,1,0:T(8,128)(2,1)} collective-permute-done((bf16[2,192,1024]{2,1,0:T(8,128)(2,1)S(1)}, bf16[2,192,1024]{2,1,0:T(8,128)(2,1)}, u32[]{:S(2)}, u32[]{:S(2)}) %collective-permute-start.3) | collective-permute-done | bytes 786464 | tf_op jit(solution)/shard_map/ppermute | solution.py:14
  41.4 1.2 %slice_bitcast_fusion = (bf16[24,8,8,128]{3,1,2,0:T(8,128)(2,1)S(1)}, bf16[24,8,8,128]{3,1,2,0:T(8,128)(2,1)S(1)}) fusion(bf16[2,192,1024]{2,1,0:T(8,128)(2,1)} %collective-permute-done.3), kind=kLoop, calls=%fused_computation.63 | loop fusion | bytes 1572864
  42.7 1.7 %fusion.14 = (f32[8,4,192]{2,1,0:T(4,128)S(1)}, f32[8,192,192,4]{2,1,3,0:T(8,128)S(1)}) fusion(pred[192,192]{0,1:T(8,128)(4,1)S(1)} %get-tuple-element.26, bf16[192,8,4,128]{3,2,1,0:T(4,128)(2,1)S(1)} %reshape.169, bf16[192,8,128,1]{2,1,0,3:T(8,128)(2,1)S(1)} %bitcast.119), kind=kOutput, calls=%fused_computation.24 | convolution fusion | flops 305522688 | bytes 6746112 | tf_op jit(solution)/shard_map/tkgd,ukd->kgtu/dot_general | solution.py:47
  44.5 1.0 %collective-permute-start.2 = (bf16[2,192,1024]{2,1,0:T(8,128)(2,1)S(1)}, bf16[2,192,1024]{2,1,0:T(8,128)(2,1)S(1)}, u32[]{:S(2)}, u32[]{:S(2)}) collective-permute-start(bf16[2,192,1024]{2,1,0:T(8,128)(2,1)S(1)} %collective-permute-done.1), channel_id=1, source_target_pairs={{31,0},{0,1},{1,2},{2,3},{3,4},{4,5},{5,6},{6,7},{7,8},{8,9},{9,10... | collective-permute-start | bytes 2359304 | tf_op jit(solution)/shard_map/ppermute | solution.py:14
  45.5 1.7 %fusion.11 = (f32[8,4,192]{2,1,0:T(4,128)S(1)}, f32[8,192,192,4]{2,1,3,0:T(8,128)S(1)}) fusion(pred[192,192]{0,1:T(8,128)(4,1)S(1)} %get-tuple-element.23, bf16[192,8,4,128]{3,2,1,0:T(4,128)(2,1)S(1)} %reshape.169, bf16[192,8,128,1]{2,1,0,3:T(8,128)(2,1)S(1)} %bitcast.117), kind=kOutput, calls=%fused_computation.21 | convolution fusion | flops 305522688 | bytes 6746112 | tf_op jit(solution)/shard_map/tkgd,ukd->kgtu/dot_general | solution.py:47
  47.6 1.7 %fusion.12 = (f32[8,4,192]{2,1,0:T(4,128)S(1)}, f32[8,192,192,4]{2,1,3,0:T(8,128)S(1)}) fusion(pred[192,192]{0,1:T(8,128)(4,1)S(1)} %get-tuple-element.24, bf16[192,8,4,128]{3,2,1,0:T(4,128)(2,1)S(1)} %reshape.169, bf16[192,8,128,1]{2,1,0,3:T(8,128)(2,1)S(1)} %bitcast.121), kind=kOutput, calls=%fused_computation.22 | convolution fusion | flops 305522688 | bytes 6746112 | tf_op jit(solution)/shard_map/tkgd,ukd->kgtu/dot_general | solution.py:47
  49.3 9.0 %collective-permute-done.2 = bf16[2,192,1024]{2,1,0:T(8,128)(2,1)S(1)} collective-permute-done((bf16[2,192,1024]{2,1,0:T(8,128)(2,1)S(1)}, bf16[2,192,1024]{2,1,0:T(8,128)(2,1)S(1)}, u32[]{:S(2)}, u32[]{:S(2)}) %collective-permute-start.2) | collective-permute-done | bytes 786464 | tf_op jit(solution)/shard_map/ppermute | solution.py:14
  58.5 4.3 %fusion.13 = (f32[8,4,192]{2,1,0:T(4,128)S(1)}, f32[8,192,192,4]{2,1,3,0:T(8,128)}) fusion(pred[192,192]{0,1:T(8,128)(4,1)S(1)} %get-tuple-element.25, bf16[192,8,4,128]{3,2,1,0:T(4,128)(2,1)S(1)} %reshape.169, bf16[192,8,128,1]{2,1,0,3:T(8,128)(2,1)S(1)} %bitcast.120), kind=kOutput, calls=%fused_computation.23 | convolution fusion | flops 305522688 | bytes 6746112 | tf_op jit(solution)/shard_map/tkgd,ukd->kgtu/dot_general | solution.py:47
  62.8 3.5 %fusion.21 = f32[8,4,192,128]{3,2,1,0:T(8,128)} fusion(f32[8,192,192,4]{2,1,3,0:T(8,128)S(1)} %get-tuple-element.37, f32[8,4,192]{2,1,0:T(4,128)S(1)} %bitcast.136, pred[192,192]{0,1:T(8,128)(4,1)S(1)} %get-tuple-element.23, bf16[192,8,128,1]{2,1,0,3:T(8,128)(2,1)S(1)} %bitcast.128), kind=kOutput, calls=%fused_computation.28 | convolution fusion | flops 306708480 | bytes 8318976 | tf_op jit(solution)/shard_map/kgtu,ukd->kgtd/dot_general | solution.py:66
  66.3 3.5 %fusion.19 = f32[8,4,192,128]{3,2,1,0:T(8,128)} fusion(f32[8,192,192,4]{2,1,3,0:T(8,128)S(1)} %get-tuple-element.33, f32[8,4,192]{2,1,0:T(4,128)S(1)} %bitcast.137, pred[192,192]{0,1:T(8,128)(4,1)S(1)} %get-tuple-element.24, bf16[192,8,128,1]{2,1,0,3:T(8,128)(2,1)S(1)} %bitcast.129), kind=kOutput, calls=%fused_computation.27 | convolution fusion | flops 306708480 | bytes 8318976 | tf_op jit(solution)/shard_map/kgtu,ukd->kgtd/dot_general | solution.py:66
  69.7 6.2 %fusion.17 = f32[8,4,192,128]{3,2,1,0:T(8,128)} fusion(f32[8,192,192,4]{2,1,3,0:T(8,128)} %get-tuple-element.31, f32[8,4,192]{2,1,0:T(4,128)S(1)} %bitcast.138, pred[192,192]{0,1:T(8,128)(4,1)S(1)} %get-tuple-element.25, bf16[192,8,128,1]{2,1,0,3:T(8,128)(2,1)S(1)} %bitcast.130), kind=kOutput, calls=%fused_computation.26 | convolution fusion | flops 306708480 | bytes 8318976 | tf_op jit(solution)/shard_map/kgtu,ukd->kgtd/dot_general | solution.py:66
  76.0 10.1 %fusion.2 = (f32[8,4,192]{2,1,0:T(4,128)S(1)}, f32[8,4,192]{2,1,0:T(4,128)S(1)}, f32[8,4,192]{2,1,0:T(4,128)S(1)}, f32[8,4,192]{2,1,0:T(4,128)S(1)}, f32[8,4,192]{2,1,0:T(4,128)S(1)}) fusion(f32[8,192,192,4]{2,1,3,0:T(8,128)S(1)} %get-tuple-element.37, f32[8,4,192]{2,1,0:T(4,128)S(1)} %bitcast.139, pred[192,192]{0,1:T(8,128)(4,1)S(1)} %get-tuple-element.23, ...), kind=kLoop, calls=%fused_computation.12 | loop fusion | flops 23562240 | bytes 23924736 | tf_op jit(solution)/shard_map/reduce_sum | solution.py:63
  86.1 1.8 %fusion.15 = f32[8,4,192,128]{3,2,1,0:T(8,128)S(1)} fusion(f32[8,192,192,4]{2,1,3,0:T(8,128)S(1)} %get-tuple-element.29, f32[8,4,192]{2,1,0:T(4,128)S(1)} %bitcast.140, pred[192,192]{0,1:T(8,128)(4,1)S(1)} %get-tuple-element.26, bf16[192,8,128,1]{2,1,0,3:T(8,128)(2,1)S(1)} %bitcast.127), kind=kOutput, calls=%fused_computation.25 | convolution fusion | flops 306708480 | bytes 8318976 | tf_op jit(solution)/shard_map/kgtu,ukd->kgtd/dot_general | solution.py:66
  89.8 2.8 %fusion.25 = bf16[192,8,4,128]{3,0,2,1:T(8,128)(2,1)S(1)} fusion(f32[8,4,192,128]{3,2,1,0:T(8,128)S(1)} %fusion.15, f32[8,4,192,128]{3,2,1,0:T(8,128)S(1)} %copy-done.2, f32[8,4,192,128]{3,2,1,0:T(8,128)S(1)} %copy-done.1, f32[8,4,192,128]{3,2,1,0:T(8,128)S(1)} %copy-done, f32[192,8,4]{0,2,1:T(4,128)S(1)} %add_bitcast_fusion, ...), kind=kOutput, calls=%fused_computation.31 | convolution fusion | flops 311427072 | bytes 19353600 | tf_op jit(solution)/shard_map/kgtu,ukd->kgtd/dot_general | solution.py:66
  92.6 1.2 %copy.37 = bf16[192,8,4,128]{3,2,1,0:T(4,128)(2,1)S(1)} copy(bf16[192,8,4,128]{3,0,2,1:T(8,128)(2,1)S(1)} %fusion.25) | data formatting | bytes 3145728 | tf_op jit(solution)/shard_map/convert_element_type | solution.py:73
  93.9 2.4 %convert_element_type.27 = bf16[192,4096]{1,0:T(8,128)(2,1)} reshape(bf16[192,8,4,128]{3,2,1,0:T(4,128)(2,1)S(1)} %copy.37) | data formatting | bytes 3145728 | tf_op jit(solution)/shard_map/convert_element_type | solution.py:73
  (31 shorter events, 3.5 us)
Async XLA Ops:
  1.2 15.0 %collective-permute-start = (bf16[2,192,1024]{2,1,0:T(8,128)(2,1)S(1)}, bf16[2,192,1024]{2,1,0:T(8,128)(2,1)S(1)}, u32[]{:S(2)}, u32[]{:S(2)}) collective-permute-start(bf16[2,192,1024]{2,1,0:T(8,128)(2,1)S(1)} %pad_maximum_fusion), channel_id=1, source_target_pairs={{31,0},{0,1},{1,2},{2,3},{3,4},{4,5},{5,6},{6,7},{7,8},{8,9},{9,10... | collective-permute-start | bytes 2359304 | tf_op jit(solution)/shard_map/ppermute | solution.py:14
  1.3 40.1 %collective-permute-start.3 = (bf16[2,192,1024]{2,1,0:T(8,128)(2,1)S(1)}, bf16[2,192,1024]{2,1,0:T(8,128)(2,1)}, u32[]{:S(2)}, u32[]{:S(2)}) collective-permute-start(bf16[2,192,1024]{2,1,0:T(8,128)(2,1)S(1)} %pad_maximum_fusion), channel_id=1, source_target_pairs={{224,0},{0,32},{32,64},{64,96},{96,128},{128,160},{160,192},{192,2... | collective-permute-start | bytes 2359304 | tf_op jit(solution)/shard_map/ppermute | solution.py:14
  16.2 28.3 %collective-permute-start.1 = (bf16[2,192,1024]{2,1,0:T(8,128)(2,1)S(1)}, bf16[2,192,1024]{2,1,0:T(8,128)(2,1)S(1)}, u32[]{:S(2)}, u32[]{:S(2)}) collective-permute-start(bf16[2,192,1024]{2,1,0:T(8,128)(2,1)S(1)} %collective-permute-done), channel_id=1, source_target_pairs={{31,0},{0,1},{1,2},{2,3},{3,4},{4,5},{5,6},{6,7},{7,8},{8,9},{9,10... | collective-permute-start | bytes 2359304 | tf_op jit(solution)/shard_map/ppermute | solution.py:14
  44.5 13.8 %collective-permute-start.2 = (bf16[2,192,1024]{2,1,0:T(8,128)(2,1)S(1)}, bf16[2,192,1024]{2,1,0:T(8,128)(2,1)S(1)}, u32[]{:S(2)}, u32[]{:S(2)}) collective-permute-start(bf16[2,192,1024]{2,1,0:T(8,128)(2,1)S(1)} %collective-permute-done.1), channel_id=1, source_target_pairs={{31,0},{0,1},{1,2},{2,3},{3,4},{4,5},{5,6},{6,7},{7,8},{8,9},{9,10... | collective-permute-start | bytes 2359304 | tf_op jit(solution)/shard_map/ppermute | solution.py:14
  86.1 1.9 %copy-start = (f32[8,4,192,128]{3,2,1,0:T(8,128)S(1)}, f32[8,4,192,128]{3,2,1,0:T(8,128)}, u32[]{:S(2)}) copy-start(f32[8,4,192,128]{3,2,1,0:T(8,128)} %fusion.21) | copy-start | bytes 9437188
  86.1 2.8 %copy-start.1 = (f32[8,4,192,128]{3,2,1,0:T(8,128)S(1)}, f32[8,4,192,128]{3,2,1,0:T(8,128)}, u32[]{:S(2)}) copy-start(f32[8,4,192,128]{3,2,1,0:T(8,128)} %fusion.19) | copy-start | bytes 9437188
  86.1 3.7 %copy-start.2 = (f32[8,4,192,128]{3,2,1,0:T(8,128)S(1)}, f32[8,4,192,128]{3,2,1,0:T(8,128)}, u32[]{:S(2)}) copy-start(f32[8,4,192,128]{3,2,1,0:T(8,128)} %fusion.17) | copy-start | bytes 9437188
where the time goes:
time: 96.9 us; the launch traced here: 96.3 us
  waiting for transfers between devices  38.8 us (40%)
  matrix products  28.9 us (30%)
  other arithmetic  12.8 us (13%)
  local copies, waits for them, and re-layouts  12.7 us (13%)
  starting transfers between devices  2.78 us (3%)
    ppermute x4, waiting for transfers between devices, from_behind(): return lax.ppermute(block, axis, route)  38.8 us
    dot_general x5, matrix products, on_device(): jnp.einsum('kgtu,ukd->kgtd', rounded, value_matrix, preferred_element_typ...  17.8 us
    dot_general x5, matrix products, on_device(): jnp.einsum('tkgd,ukd->kgtu', grouped_query, key_matrix, preferred_element...  11.1 us
    reduce_sum x1, other arithmetic, on_device(): row_sum = row_sum + jnp.sum(weights, axis=-1, keepdims=True)  10.1 us
    unnamed x20, local copies, waits for them, and re-layouts  5.84 us
    convert_element_type x2, local copies, waits for them, and re-layouts, on_device(): return weighted.transpose(2, 0, 1, 3).reshape(token_rows, QUERY_HEADS * H...  3.61 us
    reshape x1, local copies, waits for them, and re-layouts, on_device(): queries.reshape(token_rows, KEY_VALUE_HEADS, QUERY_HEADS // KEY_VALUE_HEA...  2.83 us
    ppermute x4, starting transfers between devices, from_behind(): return lax.ppermute(block, axis, route)  2.78 us
  transfers between devices with their start and end apart: 4, of which 3 were waited for; matrix products, arithmetic and copies ran while one was open for 16% of the time, Pallas kernels for 0%

commit v1 on v0

v1 whole, which is shorter than its diff:
```python
import jax
import jax.numpy as jnp
from jax import lax
from jax.experimental import pallas as pl
from jax.experimental.pallas import tpu as pltpu
from jax.sharding import PartitionSpec as P

MESH = pl.DeviceIdType.MESH
KVH = 8
REP = 4
D = 128
T = 96
SCALE = D ** (-0.5)
LEAD = 3
LEAD_EARLY = 5
INF = float("inf")

SLOTS = 12


def kernel(n_outer, n_inner, q_hbm, k_hbm, v_hbm, st_hbm, o_hbm, q_vm, kv, o_vm, st, diagonal,
           q_sem, own_sem, st_sem, o_sem, recv, send):
    g = lax.axis_index("outer")
    s = lax.axis_index("inner")
    g_next, g_prev = lax.rem(g + 1, n_outer), lax.rem(g + n_outer - 1, n_outer)

    def shard(distance):
        return lax.rem(s + distance + n_inner, n_inner)

    even = lax.rem(s, 2) == 0
    odd = lax.rem(s, 2) == 1

    def own_copies(h):
        columns = pl.ds(pl.multiple_of(h * D, D), D)
        return [
            pltpu.make_async_copy(
                ref.at[pl.ds(T * (1 - slot), T), columns], kv.at[h, i, slot], own_sem.at[h]
            )
            for i, ref in enumerate((k_hbm, v_hbm))
            for slot in range(2)
        ]

    @pl.loop(0, KVH)
    def _(h):
        for copy in own_copies(h):
            copy.start()

    st_copies = [
        pltpu.make_async_copy(st_hbm.at[group], st.at[i], st_sem.at[i])
        for i, group in enumerate((g, g_prev))
    ]
    for copy in st_copies:
        copy.start()
    q_copy = pltpu.make_async_copy(q_hbm, q_vm, q_sem)
    q_copy.start()

    @pl.when(s == 2)
    def _():
        kv[:, :, 7:9] = jnp.zeros((KVH, 2, 2, T, D), kv.dtype)

    @pl.when(s == 1)
    def _():
        kv[:, :, 7:8] = jnp.zeros((KVH, 2, 1, T, D), kv.dtype)

    half = n_inner // 2
    at_end = lax.rem(s, half) >= half - 2
    at_start = lax.rem(s, half) < 2
    flip = lax.rem(s + half, n_inner)
    ring_on = lax.rem(s + 2, half) + half * (s // half)
    ring_back = lax.rem(s + half - 2, half) + half * (s // half)
    last, lends = s >= n_inner - 2, at_end & (s < half)
    before_last = s == n_inner - 4

    def detours(h):
        return lax.rem(h, 3) == 1

    barrier = pltpu.get_barrier_semaphore()

    def greet(group, inner):
        pl.semaphore_signal(barrier, inc=1, device_id=(group, inner), device_id_type=MESH)

    greet(g_prev, s)
    greet(g, shard(-2))
    greet(g, shard(-1))

    @pl.when(even)
    def _():
        greet(g, shard(1))

    @pl.when(s < 2)
    def _():
        greet(g, ring_back)

    @pl.when(s == 0)
    def _():
        greet(g, shard(-4))

    @pl.when(lends)
    def _():
        greet(g, flip)

    more = last | lends | before_last

    @pl.when(even & jnp.logical_not(more))
    def _():
        pl.semaphore_wait(barrier, 3)

    @pl.when((even & more) | (odd & jnp.logical_not(more)))
    def _():
        pl.semaphore_wait(barrier, 4)

    @pl.when(odd & more)
    def _():
        pl.semaphore_wait(barrier, 5)

    def remote(h, src, dst, sem, target):
        return pltpu.make_async_remote_copy(
            src_ref=kv.at[h, :, src],
            dst_ref=kv.at[h, :, dst],
            send_sem=send.at[sem, h],
            recv_sem=recv.at[dst, h],
            device_id=target,
            device_id_type=MESH,
        )

    def to_next_group(h):
        return pltpu.make_async_remote_copy(
            src_ref=kv.at[h, :, pl.ds(0, 2)],
            dst_ref=kv.at[h, :, pl.ds(5, 2)],
            send_sem=send.at[0, h],
            recv_sem=recv.at[5, h],
            device_id=(g_next, s),
            device_id_type=MESH,
        )

    me = (g, s)
    two_on, one_on, one_back = (g, shard(2)), (g, shard(1)), (g, shard(-1))
    via, beside = (g, flip), (g, ring_on)
    starts = s < 2

    def first(h):
        detour = last & detours(h)
        straight = jnp.logical_not(detour)
        return [
            (straight, 1, 3, 1, two_on),
            (last & straight, 0, 8, 2, two_on),
            (detour, 1, 11, 1, via),
            (detour, 0, 10, 2, via),
            (even, 1, 2, 3, one_on),
            (s == n_inner - 3, 0, 7, 2, one_back),
        ]

    passed = [
        (None, 3, 4, 4, one_on),
        (s == 0, 8, 9, 5, one_on),
        (odd, 3, 2, 6, one_back),
        (s == 1, 8, 7, 7, one_back),
    ]
    passed_high = [
        (s == 0, 7, 9, 8, two_on),
        (before_last, 7, 9, 8, (g, shard(4))),
    ]
    between = [(None, 11, 3, 9, beside), (None, 10, 8, 10, beside)]

    def each(table, h, act):
        for condition, *entry in table:
            if condition is None:
                act(remote(h, *entry))
            else:
                @pl.when(condition)
                def _(entry=entry):
                    act(remote(h, *entry))

    def send_own(h):
        pltpu.make_async_copy(kv.at[h, :, pl.ds(0, 2)], kv.at[h, :, pl.ds(0, 2)], own_sem.at[h]).wait()
        each(first(h), h, lambda copy: copy.start())

    def send_on(h):
        to_next_group(h).start()

    for h in range(LEAD):
        send_own(h)
        send_on(h)

    early = lax.rem(s, half) >= half - 4

    @pl.when(early)
    def _():
        @pl.loop(LEAD, LEAD_EARLY)
        def _(h):
            send_own(h)

    def send_ahead(h):
        @pl.when(jnp.logical_not(early) & (h + LEAD < KVH))
        def _():
            send_own(h + LEAD)

        @pl.when(early & (h + LEAD_EARLY < KVH))
        def _():
            send_own(h + LEAD_EARLY)

        @pl.when(h + LEAD < KVH)
        def _():
            send_on(h + LEAD)

    def arrived(h, dst):
        remote(h, dst, dst, 0, me).wait_recv()

    def pass_on(h):
        arrived(h, 3)

        @pl.when(starts)
        def _():
            arrived(h, 8)

        each(passed, h, lambda copy: copy.start())

    def pass_high(h):
        arrived(h, 7)
        each(passed_high, h, lambda copy: copy.start())

    def relay(h):
        @pl.when(lends & detours(h))
        def _():
            arrived(h, 11)
            arrived(h, 10)
            each(between, h, lambda copy: copy.start())

    seam = at_end | starts
    for h in range(3):
        relay(h)
    pass_on(0)

    @pl.when(seam)
    def _():
        pass_on(1)

    @pl.when((s == 0) | before_last)
    def _():
        pass_high(0)

    @pl.when(before_last)
    def _():
        pass_high(1)

    for copy in st_copies:
        copy.wait()
    other = jnp.where(st[1, 0:1, 0:1] < st[0, 0:1, 0:1], INF, -INF).astype(jnp.float32)
    row = lax.broadcasted_iota(jnp.int32, (T, REP * T), 0)
    query = lax.rem(lax.broadcasted_iota(jnp.int32, (T, REP * T), 1), T)
    diagonal[...] = jnp.where(row <= query, INF, -INF).astype(jnp.float32)

    q_copy.wait()

    def columns(h, r):
        return pl.ds(pl.multiple_of(h * (REP * D) + r * D, D), D)

    def attend(h, wrapped):
        slots = 10 if wrapped else 7
        q = jnp.concatenate(
            [q_vm[row0:row0 + T, columns(h, r)] for row0 in (0, T) for r in range(REP)], axis=0
        )
        keys = kv[h, 0, 0:slots].reshape(slots * T, D)
        values = kv[h, 1, 0:slots].reshape(slots * T, D)
        results = []
        for c in range(2 * REP * T // 256):
            scores = lax.dot_general(
                keys, q[c * 256:(c + 1) * 256], (((1,), (1,)), ((), ())), preferred_element_type=jnp.float32
            )
            blocks, sums = [], []
            for b in range(2):
                block = 2 * c + b
                high = block >= 3
                lanes = slice((block % 3) * 128, (block % 3 + 1) * 128)
                parts = [scores[slot * T:(slot + 1) * T, b * 128:(b + 1) * 128] for slot in range(slots)]
                own = 0 if high else 1
                parts[own] = jnp.minimum(parts[own], diagonal[:, lanes])
                for slot in (5, 6):
                    parts[slot] = jnp.minimum(parts[slot], other)
                for j in range(1, 4):
                    if wrapped and high:
                        parts[6 + j] = jnp.minimum(parts[6 + j], jnp.where(s < j, INF, -INF))
                    if wrapped and not high:
                        parts[1 + j] = jnp.minimum(parts[1 + j], jnp.where(s >= j, INF, -INF))
                        parts[6 + j] = None
                if not high:
                    parts[0] = None
                top = None
                for part in parts:
                    if part is not None:
                        peak = jnp.max(part, axis=0, keepdims=True)
                        top = peak if top is None else jnp.maximum(top, peak)
                total, rounded = None, []
                for part in parts:
                    if part is None:
                        rounded.append(jnp.zeros((T, 128), jnp.bfloat16))
                    else:
                        weights = jnp.exp((part - top) * SCALE)
                        here = jnp.sum(weights, axis=0, keepdims=True)
                        total = here if total is None else total + here
                        rounded.append(weights.astype(jnp.bfloat16))
                blocks.append(jnp.concatenate(rounded, axis=0))
                sums.append(total)
            weighted = lax.dot_general(
                values, jnp.concatenate(blocks, axis=1), (((0,), (0,)), ((), ())), preferred_element_type=jnp.float32
            )
            results.append((weighted / jnp.concatenate(sums, axis=1)).T.astype(o_vm.dtype))
        result = jnp.concatenate(results, axis=0)
        for half_index in range(2):
            for r in range(REP):
                start = (half_index * REP + r) * T
                o_vm[half_index * T:(half_index + 1) * T, columns(h, r)] = result[start:start + T]

    def out_copy(h):
        columns = pl.ds(pl.multiple_of(h * (REP * D), REP * D), REP * D)
        return pltpu.make_async_copy(o_vm.at[:, columns], o_hbm.at[:, columns], o_sem.at[h])

    @pl.loop(0, KVH)
    def _(h):
        send_ahead(h)

        @pl.when(h + 3 < KVH)
        def _():
            relay(h + 3)

        @pl.when(seam & (h + 2 < KVH))
        def _():
            pass_on(h + 2)

        @pl.when(jnp.logical_not(seam) & (h + 1 < KVH))
        def _():
            pass_on(h + 1)

        @pl.when((s == 0) & (h + 1 < KVH))
        def _():
            pass_high(h + 1)

        @pl.when(before_last & (h + 2 < KVH))
        def _():
            pass_high(h + 2)

        arrived(h, 2)
        arrived(h, 4)

        @pl.when(s < 3)
        def _():
            arrived(h, 9)

        to_next_group(h).wait_recv()

        @pl.when(s >= 3)
        def _():
            attend(h, False)

        @pl.when(s < 3)
        def _():
            attend(h, True)

        out_copy(h).start()

    @pl.loop(0, KVH)
    def _(h):
        to_next_group(h).wait_send()
        each(first(h), h, lambda copy: copy.wait_send())
        each(passed, h, lambda copy: copy.wait_send())
        each(passed_high, h, lambda copy: copy.wait_send())

        @pl.when(lends & detours(h))
        def _():
            each(between, h, lambda copy: copy.wait_send())

        out_copy(h).wait()


def solution(mesh):
    n_outer, n_inner = mesh.shape["outer"], mesh.shape["inner"]

    def on_device(queries, keys, values, stretch_of):
        rows, width = queries.shape
        any_space = pl.BlockSpec(memory_space=pl.ANY)
        return pl.pallas_call(
            lambda *refs: kernel(n_outer, n_inner, *refs),
            out_shape=jax.ShapeDtypeStruct((rows, width), jnp.bfloat16),
            in_specs=[any_space] * 4,
            out_specs=any_space,
            scratch_shapes=[
                pltpu.VMEM((rows, width), jnp.bfloat16),
                pltpu.VMEM((KVH, 2, SLOTS, T, D), jnp.bfloat16),
                pltpu.VMEM((rows, width), jnp.bfloat16),
                pltpu.VMEM((2, 2, n_inner), jnp.int32),
                pltpu.VMEM((T, REP * T), jnp.float32),
                pltpu.SemaphoreType.DMA,
                pltpu.SemaphoreType.DMA((KVH,)),
                pltpu.SemaphoreType.DMA((2,)),
                pltpu.SemaphoreType.DMA((KVH,)),
                pltpu.SemaphoreType.DMA((SLOTS, KVH)),
                pltpu.SemaphoreType.DMA((11, KVH)),
            ],
            compiler_params=pltpu.CompilerParams(
                collective_id=0, has_side_effects=True, vmem_limit_bytes=48 * 1024 * 1024
            ),
            cost_estimate=pl.CostEstimate(flops=2 * 10**9, bytes_accessed=6 * 10**6, transcendentals=4 * 10**6),
        )(*(
            pltpu.with_memory_space_constraint(array, pltpu.HBM)
            for array in (queries, keys, values, stretch_of.transpose(0, 2, 1))
        ))

    rows = P(("outer", "inner"), None)
    return jax.shard_map(
        on_device, mesh=mesh, in_specs=(rows, rows, rows, P()), out_specs=rows, check_vma=False
    )
```

time: 96.9 us -> 48.6 us (0.50)
  Pallas kernels: 0 us -> 47.4 us
  waiting for transfers between devices: 38.8 us -> 0 us
  matrix products: 28.9 us -> 0 us
  other arithmetic: 12.8 us -> 0 us
  local copies, waits for them, and re-layouts: 12.7 us -> 1.15 us
  starting transfers between devices: 2.78 us -> 0 us
    pallas_call x0 -> x1, Pallas kernels: none -> 47.4 us  [on_device(): pl.pallas_call(lambda *refs: kernel(n_outer, n_inner, *refs), out_shape=j...]
    ppermute x4 -> x0, waiting for transfers between devices: 38.8 us -> none  [from_behind(): return lax.ppermute(block, axis, route)]
    dot_general x10 -> x0, matrix products: 28.9 us -> none  [the longest x5 17.8 us: on_device(): jnp.einsum('kgtu,ukd->kgtd', rounded, value_matrix, preferred_element_typ...]
    reduce_sum x1 -> x0, other arithmetic: 10.1 us -> none  [on_device(): row_sum = row_sum + jnp.sum(weights, axis=-1, keepdims=True)]
    unnamed x20 -> x1, local copies, waits for them, and re-layouts: 5.84 us -> 1.15 us
    convert_element_type x2 -> x0, local copies, waits for them, and re-layouts: 3.61 us -> none  [on_device(): return weighted.transpose(2, 0, 1, 3).reshape(token_rows, QUERY_HEADS * H...]
    reshape x1 -> x0, local copies, waits for them, and re-layouts: 2.83 us -> none  [on_device(): queries.reshape(token_rows, KEY_VALUE_HEADS, QUERY_HEADS // KEY_VALUE_HEA...]
    ppermute x4 -> x0, starting transfers between devices: 2.78 us -> none  [from_behind(): return lax.ppermute(block, axis, route)]
  transfers between devices with their start and end apart: 4 -> 0, of which waited for: 3 -> 0; matrix products, arithmetic and copies ran while one was open for 16% -> 0% of each run, Pallas kernels for 0% -> 0%
where the time goes in v1:
time: 48.6 us; the launch traced here: 48.5 us
  Pallas kernels  47.4 us (98%)
  local copies, waits for them, and re-layouts  1.15 us (2%)
    pallas_call x1, Pallas kernels, on_device(): pl.pallas_call(lambda *refs: kernel(n_outer, n_inner, *refs), out_shape=j...  47.4 us
    unnamed x1, local copies, waits for them, and re-layouts  1.15 us

profile of v1, /device:TPU:2, one launch (start us, length us, event | category | flops | bytes accessed | tf_op | source)
XLA Modules:
  0.0 48.5 jit_solution(17459889769260968779)
XLA Ops:
  0.0 47.4 %shard_map.46 = bf16[192,4096]{1,0:T(8,128)(2,1)S(1)} custom-call(bf16[192,4096]{1,0:T(8,128)(2,1)} %refs_0_.1, bf16[192,1024]{1,0:T(8,128)(2,1)} %refs_1_.1, bf16[192,1024]{1,0:T(8,128)(2,1)} %refs_2_.1, s32[8,2,32]{2,1,0:T(2,128)} %bitcast.1), custom_call_target="tpu_custom_call" | custom-call | flops 2000000000 | bytes 6000000 | tf_op jit(solution)/shard_map/pallas_call | solution.py:381
  47.4 1.1 %copy.6 = bf16[192,4096]{1,0:T(8,128)(2,1)} copy(bf16[192,4096]{1,0:T(8,128)(2,1)S(1)} %shard_map.46) | data formatting | bytes 3145728

commit v2 on v1

--- a/solution.py
+++ b/solution.py
@@ -12,7 +12,7 @@
 T = 96
 SCALE = D ** (-0.5)
 LEAD = 3
-LEAD_EARLY = 5
+LEAD_EARLY = 6
 INF = float("inf")
 
 SLOTS = 12
@@ -71,8 +71,14 @@
     last, lends = s >= n_inner - 2, at_end & (s < half)
     before_last = s == n_inner - 4
 
+    rows_y = n_outer // 2
+    y_first, y_last = lax.rem(g, rows_y) == 0, lax.rem(g, rows_y) == rows_y - 1
+    turns, turned = y_last & at_start, y_first & at_start
+    far = lax.rem(g + rows_y, n_outer)
+    turn = lax.rem(g_next + rows_y, n_outer)
+
     def detours(h):
-        return lax.rem(h, 3) == 1
+        return jnp.where(y_first | y_last, lax.rem(h, 2) == 1, lax.rem(h, 3) == 1)
 
     barrier = pltpu.get_barrier_semaphore()
 
@@ -94,24 +100,21 @@
     @pl.when(s == 0)
     def _():
         greet(g, shard(-4))
+        greet(g, ring_back + 1)
 
     @pl.when(lends)
     def _():
         greet(g, flip)
 
-    more = last | lends | before_last
-
-    @pl.when(even & jnp.logical_not(more))
-    def _():
-        pl.semaphore_wait(barrier, 3)
-
-    @pl.when((even & more) | (odd & jnp.logical_not(more)))
-    def _():
-        pl.semaphore_wait(barrier, 4)
-
-    @pl.when(odd & more)
-    def _():
-        pl.semaphore_wait(barrier, 5)
+    @pl.when(turned)
+    def _():
+        greet(far, s)
+        greet(lax.rem(g + n_outer + rows_y - 1, n_outer), s)
+
+    count = 3 + lax.rem(s, 2)
+    for extra in (last, lends, before_last, turns, turned, (s == half - 1)):
+        count += extra.astype(jnp.int32)
+    pl.semaphore_wait(barrier, count)
 
     def remote(h, src, dst, sem, target):
         return pltpu.make_async_remote_copy(
@@ -123,27 +126,41 @@
             device_id_type=MESH,
         )
 
-    def to_next_group(h):
+    def pair(h, src, dst, sem, group):
         return pltpu.make_async_remote_copy(
-            src_ref=kv.at[h, :, pl.ds(0, 2)],
-            dst_ref=kv.at[h, :, pl.ds(5, 2)],
-            send_sem=send.at[0, h],
-            recv_sem=recv.at[5, h],
-            device_id=(g_next, s),
+            src_ref=kv.at[h, :, pl.ds(src, 2)],
+            dst_ref=kv.at[h, :, pl.ds(dst, 2)],
+            send_sem=send.at[sem, h],
+            recv_sem=recv.at[dst, h],
+            device_id=(group, s),
             device_id_type=MESH,
         )
+
+    def to_next_group(h, act):
+        turning = turns & (lax.rem(h, 2) == 1)
+
+        @pl.when(turning)
+        def _():
+            act(pair(h, 0, 10, 0, turn))
+
+        @pl.when(jnp.logical_not(turning))
+        def _():
+            act(pair(h, 0, 5, 0, g_next))
+
+    def from_turn(h):
+        return pair(h, 10, 5, 11, far)
 
     me = (g, s)
     two_on, one_on, one_back = (g, shard(2)), (g, shard(1)), (g, shard(-1))
     via, beside = (g, flip), (g, ring_on)
-    starts = s < 2
 
     def first(h):
         detour = last & detours(h)
         straight = jnp.logical_not(detour)
         return [
             (straight, 1, 3, 1, two_on),
-            (last & straight, 0, 8, 2, two_on),
+            (even & last & straight, 0, 8, 2, two_on),
+            (odd & last & straight, 0, 7, 2, one_on),
             (detour, 1, 11, 1, via),
             (detour, 0, 10, 2, via),
             (even, 1, 2, 3, one_on),
@@ -154,13 +171,17 @@
         (None, 3, 4, 4, one_on),
         (s == 0, 8, 9, 5, one_on),
         (odd, 3, 2, 6, one_back),
-        (s == 1, 8, 7, 7, one_back),
     ]
     passed_high = [
+        (s == 0, 7, 8, 7, one_on),
         (s == 0, 7, 9, 8, two_on),
         (before_last, 7, 9, 8, (g, shard(4))),
     ]
-    between = [(None, 11, 3, 9, beside), (None, 10, 8, 10, beside)]
+    between = [
+        (None, 11, 3, 9, beside),
+        (even, 10, 8, 10, beside),
+        (odd, 10, 7, 10, (g, ring_on - 1)),
+    ]
 
     def each(table, h, act):
         for condition, *entry in table:
@@ -176,7 +197,7 @@
         each(first(h), h, lambda copy: copy.start())
 
     def send_on(h):
-        to_next_group(h).start()
+        to_next_group(h, lambda copy: copy.start())
 
     for h in range(LEAD):
         send_own(h)
@@ -190,18 +211,25 @@
         def _(h):
             send_own(h)
 
+    lead = LEAD + turns.astype(jnp.int32)
+
+    @pl.when(turns)
+    def _():
+        send_own(LEAD)
+        send_on(LEAD)
+
     def send_ahead(h):
-        @pl.when(jnp.logical_not(early) & (h + LEAD < KVH))
-        def _():
-            send_own(h + LEAD)
+        @pl.when(jnp.logical_not(early) & (h + lead < KVH))
+        def _():
+            send_own(h + lead)
 
         @pl.when(early & (h + LEAD_EARLY < KVH))
         def _():
             send_own(h + LEAD_EARLY)
 
-        @pl.when(h + LEAD < KVH)
-        def _():
-            send_on(h + LEAD)
+        @pl.when(h + lead < KVH)
+        def _():
+            send_on(h + lead)
 
     def arrived(h, dst):
         remote(h, dst, dst, 0, me).wait_recv()
@@ -209,7 +237,7 @@
     def pass_on(h):
         arrived(h, 3)
 
-        @pl.when(starts)
+        @pl.when(s == 0)
         def _():
             arrived(h, 8)
 
@@ -226,22 +254,30 @@
             arrived(h, 10)
             each(between, h, lambda copy: copy.start())
 
-    seam = at_end | starts
-    for h in range(3):
+    def pass_turn(h):
+        @pl.when(turned & (lax.rem(h, 2) == 1))
+        def _():
+            pair(h, 10, 10, 0, g).wait_recv()
+            from_turn(h).start()
+
+    seam = at_end | (s < 2)
+    passes_high = (s == 0) | before_last
+    for h in range(4):
         relay(h)
     pass_on(0)
 
     @pl.when(seam)
     def _():
         pass_on(1)
-
-    @pl.when((s == 0) | before_last)
+        pass_on(2)
+
+    @pl.when(passes_high)
     def _():
         pass_high(0)
-
-    @pl.when(before_last)
-    def _():
         pass_high(1)
+        pass_high(2)
+
+    pass_turn(1)
 
     for copy in st_copies:
         copy.wait()
@@ -317,27 +353,31 @@
 
     @pl.loop(0, KVH)
     def _(h):
+        @pl.when(h + 4 < KVH)
+        def _():
+            relay(h + 4)
+
+        @pl.when(seam & (h + 3 < KVH))
+        def _():
+            pass_on(h + 3)
+
+        @pl.when(passes_high & (h + 3 < KVH))
+        def _():
+            pass_high(h + 3)
+
         send_ahead(h)
 
-        @pl.when(h + 3 < KVH)
-        def _():
-            relay(h + 3)
-
-        @pl.when(seam & (h + 2 < KVH))
-        def _():
-            pass_on(h + 2)
+        @pl.when(h + 2 < KVH)
+        def _():
+            pass_turn(h + 2)
 
         @pl.when(jnp.logical_not(seam) & (h + 1 < KVH))
         def _():
             pass_on(h + 1)
 
-        @pl.when((s == 0) & (h + 1 < KVH))
-        def _():
-            pass_high(h + 1)
-
-        @pl.when(before_last & (h + 2 < KVH))
-        def _():
-            pass_high(h + 2)
+        @pl.when(s == 1)
+        def _():
+            arrived(h, 8)
 
         arrived(h, 2)
         arrived(h, 4)
@@ -346,7 +386,7 @@
         def _():
             arrived(h, 9)
 
-        to_next_group(h).wait_recv()
+        pair(h, 5, 5, 0, g).wait_recv()
 
         @pl.when(s >= 3)
         def _():
@@ -360,7 +400,7 @@
 
     @pl.loop(0, KVH)
     def _(h):
-        to_next_group(h).wait_send()
+        to_next_group(h, lambda copy: copy.wait_send())
         each(first(h), h, lambda copy: copy.wait_send())
         each(passed, h, lambda copy: copy.wait_send())
         each(passed_high, h, lambda copy: copy.wait_send())
@@ -368,6 +408,10 @@
         @pl.when(lends & detours(h))
         def _():
             each(between, h, lambda copy: copy.wait_send())
+
+        @pl.when(turned & (lax.rem(h, 2) == 1))
+        def _():
+            from_turn(h).wait_send()
 
         out_copy(h).wait()
 
@@ -394,7 +438,7 @@
                 pltpu.SemaphoreType.DMA((2,)),
                 pltpu.SemaphoreType.DMA((KVH,)),
                 pltpu.SemaphoreType.DMA((SLOTS, KVH)),
-                pltpu.SemaphoreType.DMA((11, KVH)),
+                pltpu.SemaphoreType.DMA((12, KVH)),
             ],
             compiler_params=pltpu.CompilerParams(
                 collective_id=0, has_side_effects=True, vmem_limit_bytes=48 * 1024 * 1024

time: 48.6 us -> 47.1 us (0.969)
  the two profiles are of different devices: /device:TPU:2 before, /device:TPU:4 now
where the time goes in v2:
time: 47.1 us; the launch traced here: 47 us
  Pallas kernels  45.8 us (97%)
  local copies, waits for them, and re-layouts  1.15 us (2%)
    pallas_call x1, Pallas kernels, on_device(): pl.pallas_call(lambda *refs: kernel(n_outer, n_inner, *refs), out_shape=j...  45.8 us
    unnamed x1, local copies, waits for them, and re-layouts  1.15 us

profile of v2, /device:TPU:4, one launch (start us, length us, event | category | flops | bytes accessed | tf_op | source)
XLA Modules:
  0.0 47.0 jit_solution(7905632646992290181)
XLA Ops:
  0.0 45.8 %shard_map.46 = bf16[192,4096]{1,0:T(8,128)(2,1)S(1)} custom-call(bf16[192,4096]{1,0:T(8,128)(2,1)} %refs_0_.1, bf16[192,1024]{1,0:T(8,128)(2,1)} %refs_1_.1, bf16[192,1024]{1,0:T(8,128)(2,1)} %refs_2_.1, s32[8,2,32]{2,1,0:T(2,128)} %bitcast.1), custom_call_target="tpu_custom_call" | custom-call | flops 2000000000 | bytes 6000000 | tf_op jit(solution)/shard_map/pallas_call | solution.py:425
  45.8 1.1 %copy.6 = bf16[192,4096]{1,0:T(8,128)(2,1)} copy(bf16[192,4096]{1,0:T(8,128)(2,1)S(1)} %shard_map.46) | data formatting | bytes 3145728

commit v3 on v2

--- a/solution.py
+++ b/solution.py
@@ -77,6 +77,9 @@
     far = lax.rem(g + rows_y, n_outer)
     turn = lax.rem(g_next + rows_y, n_outer)
 
+    def turns_for(h):
+        return jnp.where(s < 2, lax.rem(h, 4) == 1, lax.rem(h, 2) == 1)
+
     def detours(h):
         return jnp.where(y_first | y_last, lax.rem(h, 2) == 1, lax.rem(h, 3) == 1)
 
@@ -100,7 +103,7 @@
     @pl.when(s == 0)
     def _():
         greet(g, shard(-4))
-        greet(g, ring_back + 1)
+        greet(g, shard(2))
 
     @pl.when(lends)
     def _():
@@ -112,7 +115,7 @@
         greet(lax.rem(g + n_outer + rows_y - 1, n_outer), s)
 
     count = 3 + lax.rem(s, 2)
-    for extra in (last, lends, before_last, turns, turned, (s == half - 1)):
+    for extra in (last, lends, before_last, s == 2, turns, turned):
         count += extra.astype(jnp.int32)
     pl.semaphore_wait(barrier, count)
 
@@ -137,7 +140,7 @@
         )
 
     def to_next_group(h, act):
-        turning = turns & (lax.rem(h, 2) == 1)
+        turning = turns & turns_for(h)
 
         @pl.when(turning)
         def _():
@@ -159,8 +162,7 @@
         straight = jnp.logical_not(detour)
         return [
             (straight, 1, 3, 1, two_on),
-            (even & last & straight, 0, 8, 2, two_on),
-            (odd & last & straight, 0, 7, 2, one_on),
+            (last & straight, 0, 8, 2, two_on),
             (detour, 1, 11, 1, via),
             (detour, 0, 10, 2, via),
             (even, 1, 2, 3, one_on),
@@ -169,19 +171,14 @@
 
     passed = [
         (None, 3, 4, 4, one_on),
-        (s == 0, 8, 9, 5, one_on),
+        (s < 2, 8, 9, 5, one_on),
         (odd, 3, 2, 6, one_back),
     ]
     passed_high = [
-        (s == 0, 7, 8, 7, one_on),
-        (s == 0, 7, 9, 8, two_on),
+        (s == 2, 9, 7, 8, (g, shard(-2))),
         (before_last, 7, 9, 8, (g, shard(4))),
     ]
-    between = [
-        (None, 11, 3, 9, beside),
-        (even, 10, 8, 10, beside),
-        (odd, 10, 7, 10, (g, ring_on - 1)),
-    ]
+    between = [(None, 11, 3, 9, beside), (None, 10, 8, 10, beside)]
 
     def each(table, h, act):
         for condition, *entry in table:
@@ -237,14 +234,21 @@
     def pass_on(h):
         arrived(h, 3)
 
-        @pl.when(s == 0)
+        @pl.when(s < 2)
         def _():
             arrived(h, 8)
 
         each(passed, h, lambda copy: copy.start())
 
     def pass_high(h):
-        arrived(h, 7)
+        @pl.when(s == 2)
+        def _():
+            arrived(h, 9)
+
+        @pl.when(before_last)
+        def _():
+            arrived(h, 7)
+
         each(passed_high, h, lambda copy: copy.start())
 
     def relay(h):
@@ -255,13 +259,13 @@
             each(between, h, lambda copy: copy.start())
 
     def pass_turn(h):
-        @pl.when(turned & (lax.rem(h, 2) == 1))
+        @pl.when(turned & turns_for(h))
         def _():
             pair(h, 10, 10, 0, g).wait_recv()
             from_turn(h).start()
 
     seam = at_end | (s < 2)
-    passes_high = (s == 0) | before_last
+    passes_high = (s == 2) | before_last
     for h in range(4):
         relay(h)
     pass_on(0)
@@ -275,6 +279,9 @@
     def _():
         pass_high(0)
         pass_high(1)
+
+    @pl.when(before_last)
+    def _():
         pass_high(2)
 
     pass_turn(1)
@@ -361,10 +368,14 @@
         def _():
             pass_on(h + 3)
 
-        @pl.when(passes_high & (h + 3 < KVH))
+        @pl.when(before_last & (h + 3 < KVH))
         def _():
             pass_high(h + 3)
 
+        @pl.when((s == 2) & (h + 2 < KVH))
+        def _():
+            pass_high(h + 2)
+
         send_ahead(h)
 
         @pl.when(h + 2 < KVH)
@@ -374,15 +385,15 @@
         @pl.when(jnp.logical_not(seam) & (h + 1 < KVH))
         def _():
             pass_on(h + 1)
-
-        @pl.when(s == 1)
-        def _():
-            arrived(h, 8)
 
         arrived(h, 2)
         arrived(h, 4)
 
-        @pl.when(s < 3)
+        @pl.when(s == 0)
+        def _():
+            arrived(h, 7)
+
+        @pl.when(s < 2)
         def _():
             arrived(h, 9)
 
@@ -409,7 +420,7 @@
         def _():
             each(between, h, lambda copy: copy.wait_send())
 
-        @pl.when(turned & (lax.rem(h, 2) == 1))
+        @pl.when(turned & turns_for(h))
         def _():
             from_turn(h).wait_send()
 

time: 47.1 us -> 46.2 us (0.981)
  the two profiles are of different devices: /device:TPU:4 before, /device:TPU:2 now
where the time goes in v3:
time: 46.2 us; the launch traced here: 45.8 us
  Pallas kernels  44.7 us (97%)
  local copies, waits for them, and re-layouts  1.15 us (2%)
    pallas_call x1, Pallas kernels, on_device(): pl.pallas_call(lambda *refs: kernel(n_outer, n_inner, *refs), out_shape=j...  44.7 us
    unnamed x1, local copies, waits for them, and re-layouts  1.15 us

profile of v3, /device:TPU:2, one launch (start us, length us, event | category | flops | bytes accessed | tf_op | source)
XLA Modules:
  0.0 45.8 jit_solution(12816879470161218682)
XLA Ops:
  0.0 44.7 %shard_map.46 = bf16[192,4096]{1,0:T(8,128)(2,1)S(1)} custom-call(bf16[192,4096]{1,0:T(8,128)(2,1)} %refs_0_.1, bf16[192,1024]{1,0:T(8,128)(2,1)} %refs_1_.1, bf16[192,1024]{1,0:T(8,128)(2,1)} %refs_2_.1, s32[8,2,32]{2,1,0:T(2,128)} %bitcast.1), custom_call_target="tpu_custom_call" | custom-call | flops 2000000000 | bytes 6000000 | tf_op jit(solution)/shard_map/pallas_call | solution.py:436
  44.7 1.1 %copy.6 = bf16[192,4096]{1,0:T(8,128)(2,1)} copy(bf16[192,4096]{1,0:T(8,128)(2,1)S(1)} %shard_map.46) | data formatting | bytes 3145728

commit v4 on v3

--- a/solution.py
+++ b/solution.py
@@ -13,6 +13,8 @@
 SCALE = D ** (-0.5)
 LEAD = 3
 LEAD_EARLY = 6
+LEAD_TURN = 6
+LOG2_E = 1.4426950408889634
 INF = float("inf")
 
 SLOTS = 12
@@ -208,12 +210,14 @@
         def _(h):
             send_own(h)
 
-    lead = LEAD + turns.astype(jnp.int32)
+    lead = jnp.where(turns, LEAD_TURN, LEAD)
 
     @pl.when(turns)
     def _():
-        send_own(LEAD)
-        send_on(LEAD)
+        @pl.loop(LEAD, LEAD_TURN)
+        def _(h):
+            send_own(h)
+            send_on(h)
 
     def send_ahead(h):
         @pl.when(jnp.logical_not(early) & (h + lead < KVH))
@@ -285,6 +289,7 @@
         pass_high(2)
 
     pass_turn(1)
+    pass_turn(3)
 
     for copy in st_copies:
         copy.wait()
@@ -299,14 +304,14 @@
         return pl.ds(pl.multiple_of(h * (REP * D) + r * D, D), D)
 
     def attend(h, wrapped):
-        slots = 10 if wrapped else 7
         q = jnp.concatenate(
             [q_vm[row0:row0 + T, columns(h, r)] for row0 in (0, T) for r in range(REP)], axis=0
         )
-        keys = kv[h, 0, 0:slots].reshape(slots * T, D)
-        values = kv[h, 1, 0:slots].reshape(slots * T, D)
         results = []
         for c in range(2 * REP * T // 256):
+            slots = 10 if wrapped and c > 0 else 7
+            keys = kv[h, 0, 0:slots].reshape(slots * T, D)
+            values = kv[h, 1, 0:slots].reshape(slots * T, D)
             scores = lax.dot_general(
                 keys, q[c * 256:(c + 1) * 256], (((1,), (1,)), ((), ())), preferred_element_type=jnp.float32
             )
@@ -325,7 +330,8 @@
                         parts[6 + j] = jnp.minimum(parts[6 + j], jnp.where(s < j, INF, -INF))
                     if wrapped and not high:
                         parts[1 + j] = jnp.minimum(parts[1 + j], jnp.where(s >= j, INF, -INF))
-                        parts[6 + j] = None
+                        if slots > 7:
+                            parts[6 + j] = None
                 if not high:
                     parts[0] = None
                 top = None
@@ -338,7 +344,7 @@
                     if part is None:
                         rounded.append(jnp.zeros((T, 128), jnp.bfloat16))
                     else:
-                        weights = jnp.exp((part - top) * SCALE)
+                        weights = jnp.exp2((part - top) * (SCALE * LOG2_E))
                         here = jnp.sum(weights, axis=0, keepdims=True)
                         total = here if total is None else total + here
                         rounded.append(weights.astype(jnp.bfloat16))
@@ -378,9 +384,9 @@
 
         send_ahead(h)
 
-        @pl.when(h + 2 < KVH)
-        def _():
-            pass_turn(h + 2)
+        @pl.when(h + 4 < KVH)
+        def _():
+            pass_turn(h + 4)
 
         @pl.when(jnp.logical_not(seam) & (h + 1 < KVH))
         def _():

time: 46.2 us -> 45.8 us (level)
  no operation moved by 1% of the time
where the time goes in v4:
time: 45.8 us; the launch traced here: 45.7 us
  Pallas kernels  44.5 us (97%)
  local copies, waits for them, and re-layouts  1.15 us (3%)
    pallas_call x1, Pallas kernels, on_device(): pl.pallas_call(lambda *refs: kernel(n_outer, n_inner, *refs), out_shape=j...  44.5 us
    unnamed x1, local copies, waits for them, and re-layouts  1.15 us

profile of v4, /device:TPU:2, one launch (start us, length us, event | category | flops | bytes accessed | tf_op | source)
XLA Modules:
  0.0 45.7 jit_solution(1565568970074121219)
XLA Ops:
  0.0 44.5 %shard_map.46 = bf16[192,4096]{1,0:T(8,128)(2,1)S(1)} custom-call(bf16[192,4096]{1,0:T(8,128)(2,1)} %refs_0_.1, bf16[192,1024]{1,0:T(8,128)(2,1)} %refs_1_.1, bf16[192,1024]{1,0:T(8,128)(2,1)} %refs_2_.1, s32[8,2,32]{2,1,0:T(2,128)} %bitcast.1), custom_call_target="tpu_custom_call" | custom-call | flops 2000000000 | bytes 6000000 | tf_op jit(solution)/shard_map/pallas_call | solution.py:442
  44.5 1.1 %copy.6 = bf16[192,4096]{1,0:T(8,128)(2,1)} copy(bf16[192,4096]{1,0:T(8,128)(2,1)S(1)} %shard_map.46) | data formatting | bytes 3145728

commit v5 on v4

--- a/solution.py
+++ b/solution.py
@@ -75,15 +75,14 @@
 
     rows_y = n_outer // 2
     y_first, y_last = lax.rem(g, rows_y) == 0, lax.rem(g, rows_y) == rows_y - 1
-    turns, turned = y_last & at_start, y_first & at_start
-    far = lax.rem(g + rows_y, n_outer)
-    turn = lax.rem(g_next + rows_y, n_outer)
+    turns = y_last & at_start
+    turned = y_first & (lax.rem(s, half) >= 2) & (lax.rem(s, half) < 4)
 
     def turns_for(h):
-        return jnp.where(s < 2, lax.rem(h, 4) == 1, lax.rem(h, 2) == 1)
+        return jnp.where(s < 4, lax.rem(h, 4) == 1, lax.rem(h, 2) == 1)
 
     def detours(h):
-        return jnp.where(y_first | y_last, lax.rem(h, 2) == 1, lax.rem(h, 3) == 1)
+        return jnp.where(y_last, lax.rem(h, 2) == 1, lax.rem(h, 3) == 1)
 
     barrier = pltpu.get_barrier_semaphore()
 
@@ -113,8 +112,11 @@
 
     @pl.when(turned)
     def _():
-        greet(far, s)
-        greet(lax.rem(g + n_outer + rows_y - 1, n_outer), s)
+        greet(g_prev, shard(-2))
+
+    @pl.when(y_first & at_start)
+    def _():
+        greet(g, shard(2))
 
     count = 3 + lax.rem(s, 2)
     for extra in (last, lends, before_last, s == 2, turns, turned):
@@ -131,13 +133,13 @@
             device_id_type=MESH,
         )
 
-    def pair(h, src, dst, sem, group):
+    def pair(h, src, dst, sem, target):
         return pltpu.make_async_remote_copy(
             src_ref=kv.at[h, :, pl.ds(src, 2)],
             dst_ref=kv.at[h, :, pl.ds(dst, 2)],
             send_sem=send.at[sem, h],
             recv_sem=recv.at[dst, h],
-            device_id=(group, s),
+            device_id=target,
             device_id_type=MESH,
         )
 
@@ -146,14 +148,14 @@
 
         @pl.when(turning)
         def _():
-            act(pair(h, 0, 10, 0, turn))
+            act(pair(h, 0, 10, 0, (g_next, shard(2))))
 
         @pl.when(jnp.logical_not(turning))
         def _():
-            act(pair(h, 0, 5, 0, g_next))
+            act(pair(h, 0, 5, 0, (g_next, s)))
 
     def from_turn(h):
-        return pair(h, 10, 5, 11, far)
+        return pair(h, 10, 5, 11, (g, shard(-2)))
 
     me = (g, s)
     two_on, one_on, one_back = (g, shard(2)), (g, shard(1)), (g, shard(-1))
@@ -265,7 +267,7 @@
     def pass_turn(h):
         @pl.when(turned & turns_for(h))
         def _():
-            pair(h, 10, 10, 0, g).wait_recv()
+            pair(h, 10, 10, 0, me).wait_recv()
             from_turn(h).start()
 
     seam = at_end | (s < 2)
@@ -403,7 +405,7 @@
         def _():
             arrived(h, 9)
 
-        pair(h, 5, 5, 0, g).wait_recv()
+        pair(h, 5, 5, 0, me).wait_recv()
 
         @pl.when(s >= 3)
         def _():

time: 45.8 us -> 45 us (0.983); the launches traced: 45.7 us -> 44.3 us
  Pallas kernels: 44.5 us -> 43.1 us
    pallas_call x1, Pallas kernels: 44.5 us -> 43.1 us  [on_device(): pl.pallas_call(lambda *refs: kernel(n_outer, n_inner, *refs), out_shape=j...]
where the time goes in v5:
time: 45 us; the launch traced here: 44.3 us
  Pallas kernels  43.1 us (96%)
  local copies, waits for them, and re-layouts  1.15 us (3%)
    pallas_call x1, Pallas kernels, on_device(): pl.pallas_call(lambda *refs: kernel(n_outer, n_inner, *refs), out_shape=j...  43.1 us
    unnamed x1, local copies, waits for them, and re-layouts  1.15 us

profile of v5, /device:TPU:2, one launch (start us, length us, event | category | flops | bytes accessed | tf_op | source)
XLA Modules:
  0.0 44.3 jit_solution(14216404539377759486)
XLA Ops:
  0.0 43.1 %shard_map.46 = bf16[192,4096]{1,0:T(8,128)(2,1)S(1)} custom-call(bf16[192,4096]{1,0:T(8,128)(2,1)} %refs_0_.1, bf16[192,1024]{1,0:T(8,128)(2,1)} %refs_1_.1, bf16[192,1024]{1,0:T(8,128)(2,1)} %refs_2_.1, s32[8,2,32]{2,1,0:T(2,128)} %bitcast.1), custom_call_target="tpu_custom_call" | custom-call | flops 2000000000 | bytes 6000000 | tf_op jit(solution)/shard_map/pallas_call | solution.py:444
  43.1 1.1 %copy.6 = bf16[192,4096]{1,0:T(8,128)(2,1)} copy(bf16[192,4096]{1,0:T(8,128)(2,1)S(1)} %shard_map.46) | data formatting | bytes 3145728

commit v6 on v5

--- a/solution.py
+++ b/solution.py
@@ -74,15 +74,10 @@
     before_last = s == n_inner - 4
 
     rows_y = n_outer // 2
-    y_first, y_last = lax.rem(g, rows_y) == 0, lax.rem(g, rows_y) == rows_y - 1
-    turns = y_last & at_start
-    turned = y_first & (lax.rem(s, half) >= 2) & (lax.rem(s, half) < 4)
-
-    def turns_for(h):
-        return jnp.where(s < 4, lax.rem(h, 4) == 1, lax.rem(h, 2) == 1)
+    turns = (lax.rem(g, rows_y) == rows_y - 1) & at_start
 
     def detours(h):
-        return jnp.where(y_last, lax.rem(h, 2) == 1, lax.rem(h, 3) == 1)
+        return lax.rem(h, 3) == 1
 
     barrier = pltpu.get_barrier_semaphore()
 
@@ -110,16 +105,8 @@
     def _():
         greet(g, flip)
 
-    @pl.when(turned)
-    def _():
-        greet(g_prev, shard(-2))
-
-    @pl.when(y_first & at_start)
-    def _():
-        greet(g, shard(2))
-
     count = 3 + lax.rem(s, 2)
-    for extra in (last, lends, before_last, s == 2, turns, turned):
+    for extra in (last, lends, before_last, s == 2):
         count += extra.astype(jnp.int32)
     pl.semaphore_wait(barrier, count)
 
@@ -143,19 +130,8 @@
             device_id_type=MESH,
         )
 
-    def to_next_group(h, act):
-        turning = turns & turns_for(h)
-
-        @pl.when(turning)
-        def _():
-            act(pair(h, 0, 10, 0, (g_next, shard(2))))
-
-        @pl.when(jnp.logical_not(turning))
-        def _():
-            act(pair(h, 0, 5, 0, (g_next, s)))
-
-    def from_turn(h):
-        return pair(h, 10, 5, 11, (g, shard(-2)))
+    def to_next_group(h):
+        return pair(h, 0, 5, 0, (g_next, s))
 
     me = (g, s)
     two_on, one_on, one_back = (g, shard(2)), (g, shard(1)), (g, shard(-1))
@@ -198,13 +174,13 @@
         each(first(h), h, lambda copy: copy.start())
 
     def send_on(h):
-        to_next_group(h, lambda copy: copy.start())
+        to_next_group(h).start()
 
     for h in range(LEAD):
         send_own(h)
         send_on(h)
 
-    early = lax.rem(s, half) >= half - 4
+    early = ((lax.rem(s, half) >= half - 4) | (lax.rem(s, half) < 4)) & jnp.logical_not(turns)
 
     @pl.when(early)
     def _():
@@ -263,12 +239,6 @@
             arrived(h, 11)
             arrived(h, 10)
             each(between, h, lambda copy: copy.start())
-
-    def pass_turn(h):
-        @pl.when(turned & turns_for(h))
-        def _():
-            pair(h, 10, 10, 0, me).wait_recv()
-            from_turn(h).start()
 
     seam = at_end | (s < 2)
     passes_high = (s == 2) | before_last
@@ -290,8 +260,6 @@
     def _():
         pass_high(2)
 
-    pass_turn(1)
-    pass_turn(3)
 
     for copy in st_copies:
         copy.wait()
@@ -386,10 +354,6 @@
 
         send_ahead(h)
 
-        @pl.when(h + 4 < KVH)
-        def _():
-            pass_turn(h + 4)
-
         @pl.when(jnp.logical_not(seam) & (h + 1 < KVH))
         def _():
             pass_on(h + 1)
@@ -419,7 +383,7 @@
 
     @pl.loop(0, KVH)
     def _(h):
-        to_next_group(h, lambda copy: copy.wait_send())
+        to_next_group(h).wait_send()
         each(first(h), h, lambda copy: copy.wait_send())
         each(passed, h, lambda copy: copy.wait_send())
         each(passed_high, h, lambda copy: copy.wait_send())
@@ -427,10 +391,6 @@
         @pl.when(lends & detours(h))
         def _():
             each(between, h, lambda copy: copy.wait_send())
-
-        @pl.when(turned & turns_for(h))
-        def _():
-            from_turn(h).wait_send()
 
         out_copy(h).wait()
 

time: 45 us -> 48.7 us (1.082); the launches traced: 44.3 us -> 48.6 us
  Pallas kernels: 43.1 us -> 47.4 us
    pallas_call x1, Pallas kernels: 43.1 us -> 47.4 us  [on_device(): pl.pallas_call(lambda *refs: kernel(n_outer, n_inner, *refs), out_shape=j...]
where the time goes in v6:
time: 48.7 us; the launch traced here: 48.6 us
  Pallas kernels  47.4 us (97%)
  local copies, waits for them, and re-layouts  1.15 us (2%)
    pallas_call x1, Pallas kernels, on_device(): pl.pallas_call(lambda *refs: kernel(n_outer, n_inner, *refs), out_shape=j...  47.4 us
    unnamed x1, local copies, waits for them, and re-layouts  1.15 us

profile of v6, /device:TPU:2, one launch (start us, length us, event | category | flops | bytes accessed | tf_op | source)
XLA Modules:
  0.0 48.6 jit_solution(11517267571505392307)
XLA Ops:
  0.0 47.4 %shard_map.46 = bf16[192,4096]{1,0:T(8,128)(2,1)S(1)} custom-call(bf16[192,4096]{1,0:T(8,128)(2,1)} %refs_0_.1, bf16[192,1024]{1,0:T(8,128)(2,1)} %refs_1_.1, bf16[192,1024]{1,0:T(8,128)(2,1)} %refs_2_.1, s32[8,2,32]{2,1,0:T(2,128)} %bitcast.1), custom_call_target="tpu_custom_call" | custom-call | flops 2000000000 | bytes 6000000 | tf_op jit(solution)/shard_map/pallas_call | solution.py:404
  47.5 1.1 %copy.6 = bf16[192,4096]{1,0:T(8,128)(2,1)} copy(bf16[192,4096]{1,0:T(8,128)(2,1)S(1)} %shard_map.46) | data formatting | bytes 3145728

commit v7 on v6

--- a/solution.py
+++ b/solution.py
@@ -74,7 +74,14 @@
     before_last = s == n_inner - 4
 
     rows_y = n_outer // 2
+    y_first = lax.rem(g, rows_y) == 0
     turns = (lax.rem(g, rows_y) == rows_y - 1) & at_start
+    far, far_next = lax.rem(g + rows_y, n_outer), lax.rem(g_next + rows_y, n_outer)
+
+    turned = (lax.rem(g, rows_y) == rows_y - 1) & (lax.rem(s, half) // 2 == 1)
+
+    def turns_for(h):
+        return lax.rem(h, 2) == 1
 
     def detours(h):
         return lax.rem(h, 3) == 1
@@ -105,8 +112,16 @@
     def _():
         greet(g, flip)
 
+    @pl.when(turned)
+    def _():
+        greet(far, shard(-2))
+
+    @pl.when(y_first & at_start)
+    def _():
+        greet(lax.rem(g_prev + rows_y, n_outer), shard(2))
+
     count = 3 + lax.rem(s, 2)
-    for extra in (last, lends, before_last, s == 2):
+    for extra in (last, lends, before_last, s == 2, turns, turned):
         count += extra.astype(jnp.int32)
     pl.semaphore_wait(barrier, count)
 
@@ -130,8 +145,19 @@
             device_id_type=MESH,
         )
 
-    def to_next_group(h):
-        return pair(h, 0, 5, 0, (g_next, s))
+    def to_next_group(h, act):
+        @pl.when(turns & turns_for(h))
+        def _():
+            act(pair(h, 0, 10, 0, (far, shard(2))))
+
+        @pl.when(jnp.logical_not(turns & turns_for(h)))
+        def _():
+            act(pair(h, 0, 5, 0, (g_next, s)))
+
+    def from_turn(h, act):
+        @pl.when(turned & turns_for(h))
+        def _():
+            act(pair(h, 10, 5, 11, (far_next, shard(-2))))
 
     me = (g, s)
     two_on, one_on, one_back = (g, shard(2)), (g, shard(1)), (g, shard(-1))
@@ -174,7 +200,7 @@
         each(first(h), h, lambda copy: copy.start())
 
     def send_on(h):
-        to_next_group(h).start()
+        to_next_group(h, lambda copy: copy.start())
 
     for h in range(LEAD):
         send_own(h)
@@ -239,6 +265,13 @@
             arrived(h, 11)
             arrived(h, 10)
             each(between, h, lambda copy: copy.start())
+
+    def pass_turn(h):
+        @pl.when(turned & turns_for(h))
+        def _():
+            pair(h, 10, 10, 0, me).wait_recv()
+
+        from_turn(h, lambda copy: copy.start())
 
     seam = at_end | (s < 2)
     passes_high = (s == 2) | before_last
@@ -260,6 +293,8 @@
     def _():
         pass_high(2)
 
+
+    pass_turn(1)
 
     for copy in st_copies:
         copy.wait()
@@ -358,6 +393,10 @@
         def _():
             pass_on(h + 1)
 
+        @pl.when(h + 3 < KVH)
+        def _():
+            pass_turn(h + 3)
+
         arrived(h, 2)
         arrived(h, 4)
 
@@ -383,7 +422,8 @@
 
     @pl.loop(0, KVH)
     def _(h):
-        to_next_group(h).wait_send()
+        to_next_group(h, lambda copy: copy.wait_send())
+        from_turn(h, lambda copy: copy.wait_send())
         each(first(h), h, lambda copy: copy.wait_send())
         each(passed, h, lambda copy: copy.wait_send())
         each(passed_high, h, lambda copy: copy.wait_send())

time: 48.7 us -> 47.7 us (0.979)
  Pallas kernels: 47.4 us -> 46.4 us
    pallas_call x1, Pallas kernels: 47.4 us -> 46.4 us  [on_device(): pl.pallas_call(lambda *refs: kernel(n_outer, n_inner, *refs), out_shape=j...]
where the time goes in v7:
time: 47.7 us; the launch traced here: 47.6 us
  Pallas kernels  46.4 us (97%)
  local copies, waits for them, and re-layouts  1.15 us (2%)
    pallas_call x1, Pallas kernels, on_device(): pl.pallas_call(lambda *refs: kernel(n_outer, n_inner, *refs), out_shape=j...  46.4 us
    unnamed x1, local copies, waits for them, and re-layouts  1.15 us

profile of v7, /device:TPU:2, one launch (start us, length us, event | category | flops | bytes accessed | tf_op | source)
XLA Modules:
  0.0 47.6 jit_solution(8813459664775578758)
XLA Ops:
  0.0 46.4 %shard_map.46 = bf16[192,4096]{1,0:T(8,128)(2,1)S(1)} custom-call(bf16[192,4096]{1,0:T(8,128)(2,1)} %refs_0_.1, bf16[192,1024]{1,0:T(8,128)(2,1)} %refs_1_.1, bf16[192,1024]{1,0:T(8,128)(2,1)} %refs_2_.1, s32[8,2,32]{2,1,0:T(2,128)} %bitcast.1), custom_call_target="tpu_custom_call" | custom-call | flops 2000000000 | bytes 6000000 | tf_op jit(solution)/shard_map/pallas_call | solution.py:444
  46.4 1.1 %copy.6 = bf16[192,4096]{1,0:T(8,128)(2,1)} copy(bf16[192,4096]{1,0:T(8,128)(2,1)S(1)} %shard_map.46) | data formatting | bytes 3145728

commit v8 on v7

--- a/solution.py
+++ b/solution.py
@@ -81,7 +81,7 @@
     turned = (lax.rem(g, rows_y) == rows_y - 1) & (lax.rem(s, half) // 2 == 1)
 
     def turns_for(h):
-        return lax.rem(h, 2) == 1
+        return (lax.rem(h, 2) == 1) | (s >= half)
 
     def detours(h):
         return lax.rem(h, 3) == 1
@@ -294,7 +294,8 @@
         pass_high(2)
 
 
-    pass_turn(1)
+    for h in range(3):
+        pass_turn(h)
 
     for copy in st_copies:
         copy.wait()

time: 47.7 us -> 47.2 us (0.990)
  Pallas kernels: 46.4 us -> 45.7 us
    pallas_call x1, Pallas kernels: 46.4 us -> 45.7 us  [on_device(): pl.pallas_call(lambda *refs: kernel(n_outer, n_inner, *refs), out_shape=j...]
where the time goes in v8:
time: 47.2 us; the launch traced here: 46.8 us
  Pallas kernels  45.7 us (97%)
  local copies, waits for them, and re-layouts  1.15 us (2%)
    pallas_call x1, Pallas kernels, on_device(): pl.pallas_call(lambda *refs: kernel(n_outer, n_inner, *refs), out_shape=j...  45.7 us
    unnamed x1, local copies, waits for them, and re-layouts  1.15 us

profile of v8, /device:TPU:2, one launch (start us, length us, event | category | flops | bytes accessed | tf_op | source)
XLA Modules:
  0.0 46.8 jit_solution(11697895459858381266)
XLA Ops:
  0.0 45.7 %shard_map.46 = bf16[192,4096]{1,0:T(8,128)(2,1)S(1)} custom-call(bf16[192,4096]{1,0:T(8,128)(2,1)} %refs_0_.1, bf16[192,1024]{1,0:T(8,128)(2,1)} %refs_1_.1, bf16[192,1024]{1,0:T(8,128)(2,1)} %refs_2_.1, s32[8,2,32]{2,1,0:T(2,128)} %bitcast.1), custom_call_target="tpu_custom_call" | custom-call | flops 2000000000 | bytes 6000000 | tf_op jit(solution)/shard_map/pallas_call | solution.py:445
  45.7 1.1 %copy.6 = bf16[192,4096]{1,0:T(8,128)(2,1)} copy(bf16[192,4096]{1,0:T(8,128)(2,1)S(1)} %shard_map.46) | data formatting | bytes 3145728

commit v9 on v8

--- a/solution.py
+++ b/solution.py
@@ -81,7 +81,7 @@
     turned = (lax.rem(g, rows_y) == rows_y - 1) & (lax.rem(s, half) // 2 == 1)
 
     def turns_for(h):
-        return (lax.rem(h, 2) == 1) | (s >= half)
+        return (lax.rem(h, 2) == 1) | ((s >= half) & (lax.rem(h, 4) != 0))
 
     def detours(h):
         return lax.rem(h, 3) == 1

time: 47.2 us -> 43.7 us (0.926)
  the two profiles are of different devices: /device:TPU:2 before, /device:TPU:0 now
where the time goes in v9:
time: 43.7 us; the launch traced here: 43.6 us
  Pallas kernels  42.4 us (97%)
  local copies, waits for them, and re-layouts  1.15 us (3%)
    pallas_call x1, Pallas kernels, on_device(): pl.pallas_call(lambda *refs: kernel(n_outer, n_inner, *refs), out_shape=j...  42.4 us
    unnamed x1, local copies, waits for them, and re-layouts  1.15 us

profile of v9, /device:TPU:0, one launch (start us, length us, event | category | flops | bytes accessed | tf_op | source)
XLA Modules:
  0.0 43.6 jit_solution(8917871364463138179)
XLA Ops:
  0.0 42.4 %shard_map.46 = bf16[192,4096]{1,0:T(8,128)(2,1)S(1)} custom-call(bf16[192,4096]{1,0:T(8,128)(2,1)} %refs_0_.1, bf16[192,1024]{1,0:T(8,128)(2,1)} %refs_1_.1, bf16[192,1024]{1,0:T(8,128)(2,1)} %refs_2_.1, s32[8,2,32]{2,1,0:T(2,128)} %bitcast.1), custom_call_target="tpu_custom_call" | custom-call | flops 2000000000 | bytes 6000000 | tf_op jit(solution)/shard_map/pallas_call | solution.py:445
  42.4 1.1 %copy.6 = bf16[192,4096]{1,0:T(8,128)(2,1)} copy(bf16[192,4096]{1,0:T(8,128)(2,1)S(1)} %shard_map.46) | data formatting | bytes 3145728

commit v10 on v9

--- a/solution.py
+++ b/solution.py
@@ -81,7 +81,7 @@
     turned = (lax.rem(g, rows_y) == rows_y - 1) & (lax.rem(s, half) // 2 == 1)
 
     def turns_for(h):
-        return (lax.rem(h, 2) == 1) | ((s >= half) & (lax.rem(h, 4) != 0))
+        return (lax.rem(h, 4) == 1) | ((s >= half) & (lax.rem(h, 4) != 0))
 
     def detours(h):
         return lax.rem(h, 3) == 1
@@ -214,11 +214,11 @@
         def _(h):
             send_own(h)
 
-    lead = jnp.where(turns, LEAD_TURN, LEAD)
+    lead = jnp.where(turns, jnp.where(s < 2, LEAD + 1, LEAD_TURN), LEAD)
 
     @pl.when(turns)
     def _():
-        @pl.loop(LEAD, LEAD_TURN)
+        @pl.loop(LEAD, lead)
         def _(h):
             send_own(h)
             send_on(h)

time: 43.7 us -> 47 us (1.076)
  the two profiles are of different devices: /device:TPU:0 before, /device:TPU:56 now
where the time goes in v10:
time: 47 us; the launch traced here: 46.9 us
  Pallas kernels  45.7 us (97%)
  local copies, waits for them, and re-layouts  1.15 us (2%)
    pallas_call x1, Pallas kernels, on_device(): pl.pallas_call(lambda *refs: kernel(n_outer, n_inner, *refs), out_shape=j...  45.7 us
    unnamed x1, local copies, waits for them, and re-layouts  1.15 us

profile of v10, /device:TPU:56, one launch (start us, length us, event | category | flops | bytes accessed | tf_op | source)
XLA Modules:
  0.0 46.9 jit_solution(16820001208490991941)
XLA Ops:
  0.0 45.7 %shard_map.46 = bf16[192,4096]{1,0:T(8,128)(2,1)S(1)} custom-call(bf16[192,4096]{1,0:T(8,128)(2,1)} %refs_0_.1, bf16[192,1024]{1,0:T(8,128)(2,1)} %refs_1_.1, bf16[192,1024]{1,0:T(8,128)(2,1)} %refs_2_.1, s32[8,2,32]{2,1,0:T(2,128)} %bitcast.1), custom_call_target="tpu_custom_call" | custom-call | flops 2000000000 | bytes 6000000 | tf_op jit(solution)/shard_map/pallas_call | solution.py:445
  45.7 1.1 %copy.6 = bf16[192,4096]{1,0:T(8,128)(2,1)} copy(bf16[192,4096]{1,0:T(8,128)(2,1)S(1)} %shard_map.46) | data formatting | bytes 3145728

commit v11 on v9

--- a/solution.py
+++ b/solution.py
@@ -294,7 +294,7 @@
         pass_high(2)
 
 
-    for h in range(3):
+    for h in range(4):
         pass_turn(h)
 
     for copy in st_copies:
@@ -394,9 +394,9 @@
         def _():
             pass_on(h + 1)
 
-        @pl.when(h + 3 < KVH)
-        def _():
-            pass_turn(h + 3)
+        @pl.when(h + 4 < KVH)
+        def _():
+            pass_turn(h + 4)
 
         arrived(h, 2)
         arrived(h, 4)

time: 43.7 us -> 45 us (1.030)
  the two profiles are of different devices: /device:TPU:0 before, /device:TPU:32 now
where the time goes in v11:
time: 45 us; the launch traced here: 44.9 us
  Pallas kernels  43.8 us (97%)
  local copies, waits for them, and re-layouts  1.15 us (3%)
    pallas_call x1, Pallas kernels, on_device(): pl.pallas_call(lambda *refs: kernel(n_outer, n_inner, *refs), out_shape=j...  43.8 us
    unnamed x1, local copies, waits for them, and re-layouts  1.15 us

profile of v11, /device:TPU:32, one launch (start us, length us, event | category | flops | bytes accessed | tf_op | source)
XLA Modules:
  0.0 44.9 jit_solution(7109796709190375790)
XLA Ops:
  0.0 43.8 %shard_map.46 = bf16[192,4096]{1,0:T(8,128)(2,1)S(1)} custom-call(bf16[192,4096]{1,0:T(8,128)(2,1)} %refs_0_.1, bf16[192,1024]{1,0:T(8,128)(2,1)} %refs_1_.1, bf16[192,1024]{1,0:T(8,128)(2,1)} %refs_2_.1, s32[8,2,32]{2,1,0:T(2,128)} %bitcast.1), custom_call_target="tpu_custom_call" | custom-call | flops 2000000000 | bytes 6000000 | tf_op jit(solution)/shard_map/pallas_call | solution.py:445
  43.8 1.1 %copy.6 = bf16[192,4096]{1,0:T(8,128)(2,1)} copy(bf16[192,4096]{1,0:T(8,128)(2,1)S(1)} %shard_map.46) | data formatting | bytes 3145728

commit v12 on v9

--- a/solution.py
+++ b/solution.py
@@ -81,7 +81,7 @@
     turned = (lax.rem(g, rows_y) == rows_y - 1) & (lax.rem(s, half) // 2 == 1)
 
     def turns_for(h):
-        return (lax.rem(h, 2) == 1) | ((s >= half) & (lax.rem(h, 4) != 0))
+        return jnp.where(s < half, lax.rem(h, 3) != 0, lax.rem(h, 4) != 0)
 
     def detours(h):
         return lax.rem(h, 3) == 1

time: 43.7 us -> 46.2 us (1.057)
  the two profiles are of different devices: /device:TPU:0 before, /device:TPU:4 now
where the time goes in v12:
time: 46.2 us; the launch traced here: 46.1 us
  Pallas kernels  44.9 us (97%)
  local copies, waits for them, and re-layouts  1.15 us (2%)
    pallas_call x1, Pallas kernels, on_device(): pl.pallas_call(lambda *refs: kernel(n_outer, n_inner, *refs), out_shape=j...  44.9 us
    unnamed x1, local copies, waits for them, and re-layouts  1.15 us

profile of v12, /device:TPU:4, one launch (start us, length us, event | category | flops | bytes accessed | tf_op | source)
XLA Modules:
  0.0 46.1 jit_solution(7967143389762370930)
XLA Ops:
  0.0 44.9 %shard_map.46 = bf16[192,4096]{1,0:T(8,128)(2,1)S(1)} custom-call(bf16[192,4096]{1,0:T(8,128)(2,1)} %refs_0_.1, bf16[192,1024]{1,0:T(8,128)(2,1)} %refs_1_.1, bf16[192,1024]{1,0:T(8,128)(2,1)} %refs_2_.1, s32[8,2,32]{2,1,0:T(2,128)} %bitcast.1), custom_call_target="tpu_custom_call" | custom-call | flops 2000000000 | bytes 6000000 | tf_op jit(solution)/shard_map/pallas_call | solution.py:445
  45.0 1.1 %copy.6 = bf16[192,4096]{1,0:T(8,128)(2,1)} copy(bf16[192,4096]{1,0:T(8,128)(2,1)S(1)} %shard_map.46) | data formatting | bytes 3145728

commit v13 on v11

--- a/solution.py
+++ b/solution.py
@@ -294,7 +294,7 @@
         pass_high(2)
 
 
-    for h in range(4):
+    for h in range(2):
         pass_turn(h)
 
     for copy in st_copies:
@@ -394,9 +394,9 @@
         def _():
             pass_on(h + 1)
 
-        @pl.when(h + 4 < KVH)
-        def _():
-            pass_turn(h + 4)
+        @pl.when(h + 2 < KVH)
+        def _():
+            pass_turn(h + 2)
 
         arrived(h, 2)
         arrived(h, 4)

time: 45 us -> 45.2 us (level)
  the two profiles are of different devices: /device:TPU:32 before, /device:TPU:2 now
where the time goes in v13:
time: 45.2 us; the launch traced here: 45.1 us
  Pallas kernels  43.9 us (97%)
  local copies, waits for them, and re-layouts  1.15 us (3%)
    pallas_call x1, Pallas kernels, on_device(): pl.pallas_call(lambda *refs: kernel(n_outer, n_inner, *refs), out_shape=j...  43.9 us
    unnamed x1, local copies, waits for them, and re-layouts  1.15 us

profile of v13, /device:TPU:2, one launch (start us, length us, event | category | flops | bytes accessed | tf_op | source)
XLA Modules:
  0.0 45.1 jit_solution(4615604708918891176)
XLA Ops:
  0.0 43.9 %shard_map.46 = bf16[192,4096]{1,0:T(8,128)(2,1)S(1)} custom-call(bf16[192,4096]{1,0:T(8,128)(2,1)} %refs_0_.1, bf16[192,1024]{1,0:T(8,128)(2,1)} %refs_1_.1, bf16[192,1024]{1,0:T(8,128)(2,1)} %refs_2_.1, s32[8,2,32]{2,1,0:T(2,128)} %bitcast.1), custom_call_target="tpu_custom_call" | custom-call | flops 2000000000 | bytes 6000000 | tf_op jit(solution)/shard_map/pallas_call | solution.py:445
  44.0 1.1 %copy.6 = bf16[192,4096]{1,0:T(8,128)(2,1)} copy(bf16[192,4096]{1,0:T(8,128)(2,1)S(1)} %shard_map.46) | data formatting | bytes 3145728

commit v14 on v9

--- a/solution.py
+++ b/solution.py
@@ -13,7 +13,7 @@
 SCALE = D ** (-0.5)
 LEAD = 3
 LEAD_EARLY = 6
-LEAD_TURN = 6
+LEAD_TURN = 8
 LOG2_E = 1.4426950408889634
 INF = float("inf")
 

time: 43.7 us -> 47.9 us (1.096)
  the two profiles are of different devices: /device:TPU:0 before, /device:TPU:4 now
where the time goes in v14:
time: 47.9 us; the launch traced here: 47.8 us
  Pallas kernels  46.6 us (97%)
  local copies, waits for them, and re-layouts  1.15 us (2%)
    pallas_call x1, Pallas kernels, on_device(): pl.pallas_call(lambda *refs: kernel(n_outer, n_inner, *refs), out_shape=j...  46.6 us
    unnamed x1, local copies, waits for them, and re-layouts  1.15 us

profile of v14, /device:TPU:4, one launch (start us, length us, event | category | flops | bytes accessed | tf_op | source)
XLA Modules:
  0.0 47.8 jit_solution(16706641358063146299)
XLA Ops:
  0.0 46.6 %shard_map.46 = bf16[192,4096]{1,0:T(8,128)(2,1)S(1)} custom-call(bf16[192,4096]{1,0:T(8,128)(2,1)} %refs_0_.1, bf16[192,1024]{1,0:T(8,128)(2,1)} %refs_1_.1, bf16[192,1024]{1,0:T(8,128)(2,1)} %refs_2_.1, s32[8,2,32]{2,1,0:T(2,128)} %bitcast.1), custom_call_target="tpu_custom_call" | custom-call | flops 2000000000 | bytes 6000000 | tf_op jit(solution)/shard_map/pallas_call | solution.py:445
  46.6 1.1 %copy.6 = bf16[192,4096]{1,0:T(8,128)(2,1)} copy(bf16[192,4096]{1,0:T(8,128)(2,1)S(1)} %shard_map.46) | data formatting | bytes 3145728
